TPU v7x, 256 devices: a whole 4x4x8 slice. The times are simulated.
256 devices in a mesh: ia: 8 (over y, core), ja: 32 (over x, z).
Axes of the slice: x: 4, y: 4, z: 8, core: 2. Of those that a mesh axis runs over, the one named last changes fastest.
Arguments:
- position: float32 [3, 1048576], P(None, ('ia', 'ja')), may hold values from -6 to 6
- velocity: float32 [3, 1048576], P(None, ('ia', 'ja')), may hold values from -4 to 4
- acceleration: float32 [3, 1048576], P(None, ('ia', 'ja')), may hold values from -4 to 4
- old_jerk: float32 [3, 1048576], P(None, ('ia', 'ja')), may hold values from -6 to 6
- star_mass: float32 [1048576], P(('ia', 'ja')), may hold values from 6.6757204e-09 to 6.67572e-06
- elapsed: float32 [1048576], P(('ia', 'ja')), may hold values from 0.05 to 1
- active: int32 [4096], P('ia'), may hold values from 0 to 1048575, as said below
Outputs:
- corrected: float32 [12, 4096], P(None, 'ia')
- potential: float32 [4096], P('ia')
Inputs may be any that keep to these rules, and one draw needn't show every extreme that they name: `active`: 4096 distinct star indices.
All inputs are finite; a program needn't handle non-finite values.
Results may differ from a plain program's by a relative error of at most 0.0003.
Values sent between devices are 32-bit elements; how exact they have to be, the bound alone decides.
A program may use at most 64 MiB of HBM per device.

v0:
```python
import jax
import jax.numpy as jnp
from jax import lax
from jax.sharding import PartitionSpec as P

soft_square = 0.0001


def predict(position, velocity, acceleration, old_jerk, elapsed):
    span = elapsed[None, :]
    pos_pred = position + span * (velocity + span * (acceleration / 2.0 + span * old_jerk / 6.0))
    vel_pred = velocity + span * (acceleration + span * old_jerk / 2.0)
    return (pos_pred, vel_pred)


def interact(target_pos, target_vel, target_ids, field, field_ids):
    rows = target_pos.shape[1]
    width = field.shape[1]
    block_width = min(width, max(128, 262144 // rows))
    count = width // block_width

    def step_block(index, totals):
        block = lax.dynamic_slice_in_dim(field, index * block_width, block_width, 1)
        block_ids = lax.dynamic_slice_in_dim(field_ids, index * block_width, block_width, 0)
        offset = block[0:3, None, :] - target_pos[:, :, None]
        relvel = block[3:6, None, :] - target_vel[:, :, None]
        dist = jnp.sum(offset * offset, 0) + soft_square
        inv_root = lax.rsqrt(dist)
        distinct = block_ids[None, :] != target_ids[:, None]
        weight = jnp.where(distinct, block[6][None, :] * inv_root, 0.0)
        inv_square = inv_root * inv_root
        cube = weight * inv_square
        along = 3.0 * jnp.sum(offset * relvel, 0) * inv_square
        accel_sum = jnp.sum(cube[None] * offset, 2)
        jerk_sum = jnp.sum(cube[None] * (relvel - along[None] * offset), 2)
        return (totals[0] + accel_sum, totals[1] + jerk_sum, totals[2] - jnp.sum(weight, 1))

    start = (
        jnp.zeros((3, rows), jnp.float32),
        jnp.zeros((3, rows), jnp.float32),
        jnp.zeros((rows,), jnp.float32),
    )
    return lax.fori_loop(0, count, step_block, start)


def correct(state, span, accel_new, jerk_new):
    pos_now = state[0:3]
    vel_now = state[3:6]
    accel_old = state[6:9]
    jerk_prev = state[9:12]
    times = span[None, :]
    accel_gap = accel_old - accel_new
    second_term = -6.0 * accel_gap - times * (4.0 * jerk_prev + 2.0 * jerk_new)
    third_term = 12.0 * accel_gap + 6.0 * times * (jerk_prev + jerk_new)
    pos_new = pos_now + times * times * (second_term / 24.0 + third_term / 120.0)
    vel_new = vel_now + times * (second_term / 6.0 + third_term / 24.0)
    return jnp.concatenate([pos_new, vel_new, accel_new, jerk_new], 0)


def gather_all_state(picked, picked_span):
    return lax.psum((picked, picked_span), ("ia", "ja"))


def local(position, velocity, acceleration, old_jerk, star_mass, elapsed, active):
    row_index = lax.axis_index("ia")
    col_index = lax.axis_index("ja")
    count_ja = lax.axis_size("ja")
    star_dev = position.shape[1]
    act_dev = active.shape[0]
    pos_pred, vel_pred = predict(position, velocity, acceleration, old_jerk, elapsed)
    first_star = (row_index * count_ja + col_index) * star_dev
    all_ids = lax.all_gather(active, "ia", axis=0, tiled=True)
    local_spot = all_ids - first_star
    owned_mask = (local_spot >= 0) & (local_spot < star_dev)
    clipped = jnp.clip(local_spot, 0, star_dev - 1)
    packed = jnp.concatenate([pos_pred, vel_pred, acceleration, old_jerk], 0)
    picked = jnp.where(owned_mask[None, :], jnp.take(packed, clipped, axis=1), 0.0)
    picked_span = jnp.where(owned_mask, jnp.take(elapsed, clipped), 0.0)
    field = jnp.concatenate([pos_pred, vel_pred, star_mass[None, :]], 0)
    all_state, all_span = gather_all_state(picked, picked_span)
    own_state = lax.dynamic_slice_in_dim(all_state, row_index * act_dev, act_dev, 1)
    own_span = lax.dynamic_slice_in_dim(all_span, row_index * act_dev, act_dev, 0)
    piece = lax.all_gather(field, "ia", axis=1, tiled=True)
    position_in = jnp.arange(piece.shape[1], dtype=jnp.int32)
    block_row = position_in // star_dev
    piece_ids = (block_row * count_ja + col_index) * star_dev + position_in % star_dev
    accel_sum, jerk_sum, pot_sum = interact(
        own_state[0:3], own_state[3:6], active, piece, piece_ids
    )
    accel_new, jerk_new, potential = lax.psum((accel_sum, jerk_sum, pot_sum), "ja")
    corrected = correct(own_state, own_span, accel_new, jerk_new)
    return (corrected, potential)


def solution(mesh):
    placed = (
        P(None, ("ia", "ja")),
        P(None, ("ia", "ja")),
        P(None, ("ia", "ja")),
        P(None, ("ia", "ja")),
        P(("ia", "ja")),
        P(("ia", "ja")),
        P("ia"),
    )
    return jax.shard_map(
        local, mesh=mesh, in_specs=placed, out_specs=(P(None, "ia"), P("ia")), check_vma=False
    )
```

profile of v0, /device:TPU:8, one launch (start us, length us, event | category | flops | bytes accessed | tf_op | source)
XLA Modules:
  0.0 671.7 jit_solution(1378869710933908148)
XLA Ops:
  7.2 11.9 %all-gather = s32[8,1,512]{2,1,0:T(1,128)S(1)} all-gather(s32[1,1,512]{2,1,0:T(1,128)} %bitcast.13), channel_id=1, replica_groups=mesh['ia'=8,'ja'=32] {'ia'}, dimensions={0}, use_global_device_ids=true | all-gather | bytes 18432 | tf_op jit(solution)/shard_map/all_gather | solution.py:72
  19.4 23.0 %gather_fusion.1 = f32[4096]{0:T(1024)S(1)} fusion(f32[4096]{0:T(1024)S(1)} %copy-done, s32[4096]{0:T(1024)S(1)} %fusion.17), kind=kCustom, calls=%fused_computation.1 | custom fusion | bytes 49152 | tf_op jit(solution)/shard_map/jit(_take)/gather | solution.py:78
  43.2 14.1 %gather_fusion = f32[4096,12]{1,0:T(8,128)} fusion(f32[12,4096]{0,1:T(8,128)S(1)} %copy.66, s32[4096]{0:T(1024)S(1)} %fusion.17), kind=kCustom, calls=%fused_computation | custom fusion | bytes 409600 | tf_op jit(solution)/shard_map/jit(_take)/gather | solution.py:77
  57.3 2.2 copy.67
  60.4 79.0 %psum.36 = f32[4096]{0:T(1024)S(1)} all-reduce(f32[4096]{0:T(1024)S(1)} %get-tuple-element.261), channel_id=1, replica_groups=mesh['ia'=8,'ja'=32] {'ia','ja'}, use_global_device_ids=true, to_apply=%region_1.2 | all-reduce | flops 4096 | bytes 32768 | tf_op jit(solution)/shard_map/psum | solution.py:61
  139.5 13.9 %all_gather.7 = f32[7,32768]{1,0:T(8,128)S(1)} all-gather(f32[7,4096]{1,0:T(8,128)S(1)} %pad_maximum_fusion.1), channel_id=1, replica_groups=mesh['ia'=8,'ja'=32] {'ia'}, dimensions={1}, use_global_device_ids=true | all-gather | bytes 1032192 | tf_op jit(solution)/shard_map/all_gather | solution.py:83
  153.5 159.4 %all-reduce.3.cloned.1.call-done = f32[12,4096]{1,0:T(8,128)} async-done(((f32[12,4096]{1,0:T(8,128)}), f32[12,4096]{1,0:T(8,128)}) %all-reduce.3.cloned.1.call-update) | async-done | bytes 196624 | tf_op jit(solution)/shard_map/psum | solution.py:61
  313.7 209.7 %while.18 = (s32[]{:T(128)}, f32[3,512]{1,0:T(4,128)S(1)}, f32[3,512]{1,0:T(4,128)S(1)}, f32[512]{0:T(512)S(1)}, s32[32768]{0:T(1024)S(1)}, /*index=5*/s32[512]{...) while((s32[]{:T(128)}, f32[3,512]{1,0:T(4,128)S(1)}, ...), condition=%wide.region_8.9_spmd.clone, body=%wide.region_2.8_spmd.clone.sunk | while | flops 12848649 | bytes 8534262 | solution.py:43
  321.9 1.6 fusion.25
  325.2 1.6 fusion.25
  338.3 1.6 fusion.25
  341.6 1.6 fusion.25
  351.4 1.6 fusion.25
  354.7 1.6 fusion.25
  358.0 1.6 fusion.25
  367.8 1.6 fusion.25
  371.1 1.6 fusion.25
  384.2 1.6 fusion.25
  387.5 1.6 fusion.25
  400.6 1.6 fusion.25
  403.8 1.6 fusion.25
  413.7 1.6 fusion.25
  416.9 1.6 fusion.25
  523.4 139.9 %all-reduce = (f32[3,512]{1,0:T(4,128)S(1)}, f32[3,512]{1,0:T(4,128)S(1)}, f32[512]{0:T(512)}) all-reduce(f32[3,512]{1,0:T(4,128)S(1)} %get-tuple-element.159, f32[3,512]{1,0:T(4,128)S(1)} %get-tuple-element.158, f32[512]{0:T(512)S(1)} %get-tuple-element.160), channel_id=1, replica_groups=mesh['ia'=8,'ja'=32] {'ja'}, use_global_device_ids=true, to_apply=%region_10.11 | all-reduce | flops 3584 | bytes 28672 | tf_op jit(solution)/shard_map/psum | solution.py:90
  (533 shorter events, 188.1 us)
Async XLA Ops:
  7.2 12.1 %copy-start = (f32[4096]{0:T(1024)S(1)}, f32[4096]{0:T(1024)}, u32[]{:S(2)}) copy-start(f32[4096]{0:T(1024)} %param.14) | copy-start | bytes 49156
  7.2 305.7 %all-reduce.3.cloned.1.call-start = ((), (), s32[]{:S(2)}) async-start(), calls=%async_computation | async-start | bytes 524288 | tf_op jit(solution)/shard_map/psum | solution.py:61
  19.3 23.1 %copy-start.1 = (f32[3,4096]{1,0:T(4,128)S(1)}, f32[3,4096]{1,0:T(4,128)}, u32[]{:S(2)}) copy-start(f32[3,4096]{1,0:T(4,128)} %param.11) | copy-start | bytes 147460
  19.3 23.1 %copy-start.2 = (f32[3,4096]{1,0:T(4,128)S(1)}, f32[3,4096]{1,0:T(4,128)}, u32[]{:S(2)}) copy-start(f32[3,4096]{1,0:T(4,128)} %param.12) | copy-start | bytes 147460
  19.3 23.1 %copy-start.4 = (f32[3,4096]{1,0:T(4,128)S(1)}, f32[3,4096]{1,0:T(4,128)}, u32[]{:S(2)}) copy-start(f32[3,4096]{1,0:T(4,128)} %param.9) | copy-start | bytes 147460
  19.3 23.1 %copy-start.5 = (f32[3,4096]{1,0:T(4,128)S(1)}, f32[3,4096]{1,0:T(4,128)}, u32[]{:S(2)}) copy-start(f32[3,4096]{1,0:T(4,128)} %param.10) | copy-start | bytes 147460
  57.3 82.1 %copy-start.6 = (f32[4096]{0:T(1024)S(1)}, f32[4096]{0:T(1024)}, u32[]{:S(2)}) copy-start(f32[4096]{0:T(1024)} %param.13) | copy-start | bytes 49156
  57.3 256.4 %copy-start.3 = (s32[512]{0:T(512)S(1)}, s32[512]{0:T(512)}, u32[]{:S(2)}) copy-start(s32[512]{0:T(512)} %param.15) | copy-start | bytes 6148
Sparse Core Ops, SparseCore 0:
  60.5 252.3 all-reduce.2
where the time goes:
time: 672 us
  blocking collectives  245 us (36%)
  other arithmetic  195 us (29%)
  waiting for transfers between devices  159 us (24%)
  local copies, waits for them, and re-layouts  55.7 us (8%)
  between operations  14.2 us (2%)
    psum x1, waiting for transfers between devices, gather_all_state(): return lax.psum((picked, picked_span), ('ia', 'ja'))  159 us
    psum x1, blocking collectives, local(): lax.psum((accel_sum, jerk_sum, pot_sum), 'ja')  140 us
    reduce_sum x64, other arithmetic, step_block(): jerk_sum = jnp.sum(cube[None] * (relvel - along[None] * offset), 2)  99.6 us
    psum x1, blocking collectives, gather_all_state(): return lax.psum((picked, picked_span), ('ia', 'ja'))  79 us
    reduce_sum x64, other arithmetic, step_block(): along = 3.0 * jnp.sum(offset * relvel, 0) * inv_square  61.7 us
    reduce_sum x64, other arithmetic, step_block(): jnp.sum(weight, 1)  29.3 us
    gather x1, local copies, waits for them, and re-layouts, local(): picked_span = jnp.where(owned_mask, jnp.take(elapsed, clipped), 0.0)  23 us
    gather x2, local copies, waits for them, and re-layouts, local(): jnp.take(packed, clipped, axis=1)  16.3 us
  transfers between devices with their start and end apart: 1, of which 1 were waited for; matrix products, arithmetic and copies ran while one was open for 0% of the time, Pallas kernels for 0%

commit v1 on v0

v1 whole, which is shorter than its diff:
```python
import functools

import jax
import jax.numpy as jnp
import numpy as np
from jax import lax
from jax.experimental import pallas as pl
from jax.experimental.pallas import tpu as pltpu
from jax.sharding import PartitionSpec as P

soft_square = 0.0001
self_root = float(np.float64(np.float32(soft_square)) ** -0.5)
MESH = pl.DeviceIdType.MESH
F32 = jnp.float32
BF16 = jnp.bfloat16

N_IA = 8
N_X = 4
N_Z = 8
CHUNK = 8192


def split_three(value):
    high = value.astype(BF16)
    rest = value - high.astype(F32)
    middle = rest.astype(BF16)
    low = (rest - middle.astype(F32)).astype(BF16)
    return high, middle, low


def place():
    ia = lax.axis_index("ia")
    ja = lax.axis_index("ja")
    return ia, ja, ja // N_Z, ja % N_Z


def enter(peers):
    barrier = pltpu.get_barrier_semaphore()
    for peer in peers:
        pl.semaphore_signal(barrier, inc=1, device_id=peer, device_id_type=MESH)
    pl.semaphore_wait(barrier, len(peers))


def push(src, dst, send_sem, recv_sem, peer):
    return pltpu.make_async_remote_copy(
        src_ref=src, dst_ref=dst, send_sem=send_sem, recv_sem=recv_sem,
        device_id=peer, device_id_type=MESH,
    )


def ja_peers(ia, x, z):
    along_x = [(ia, ((x + d) % N_X) * N_Z + z) for d in range(1, N_X)]
    along_z = [(ia, x * N_Z + (z + d) % N_Z) for d in range(1, N_Z)]
    return along_x, along_z


def wait_all(slots, count, send, recv, peer):
    part = slots.at[pl.ds(0, count)]
    push(part, part, send, recv, peer).wait()


def share_over_ja(x, z, part, along_x, along_z, from_z, full, sems, meanwhile=None):
    from_z[z] = part
    for d in range(1, N_Z):
        push(from_z.at[z], from_z.at[z], sems.at[0], sems.at[1], along_z[d - 1]).start()
    wait_all(from_z, N_Z - 1, sems.at[0], sems.at[1], along_z[0])
    total = from_z[0]
    for i in range(1, N_Z):
        total = total + from_z[i]
    full[x] = total
    for d in range(1, N_X):
        push(full.at[x], full.at[x], sems.at[2], sems.at[3], along_x[d - 1]).start()
    if meanwhile is not None:
        meanwhile()
    wait_all(full, N_X - 1, sems.at[2], sems.at[3], along_x[0])


def gather_kernel(
    pos_in, vel_in, acc_in, jerk_in, mass_in, elapsed_in, active_in,
    state, field,
    pos, vel, acc, jerk, mass, elapsed, active,
    ids, packed, outgoing, incoming, from_z,
    load, id_send, id_recv, part_send, part_recv, field_send, field_recv, ja_sems,
):
    ia, ja, x, z = place()
    y, core = ia // 2, ia % 2
    star_dev = pos.shape[1]
    loads = []
    for i, (src, dst) in enumerate((
        (active_in, active), (pos_in, pos), (vel_in, vel), (acc_in, acc), (jerk_in, jerk),
        (elapsed_in, elapsed), (mass_in, mass),
    )):
        c = pltpu.make_async_copy(src, dst, load.at[i])
        c.start()
        loads.append(c)
    along_x, along_z = ja_peers(ia, x, z)
    along_ia = [((ia + d) % N_IA, ja) for d in range(1, N_IA)]
    plane = [
        ((ia + d) % N_IA, ((x + e) % N_X) * N_Z + z)
        for d in range(N_IA) for e in range(N_X) if d + e > 0
    ]
    enter(plane + along_z)

    loads[0].wait()

    def send_ids(d):
        return push(active, ids.at[ia], id_send.at[d], id_recv.at[d], ((ia + d) % N_IA, ja))

    for d in range(1, N_IA):
        send_ids(d).start()
    ids[ia] = active[...]

    for c in loads[1:]:
        c.wait()
    span = elapsed[...]
    a, j = acc[...], jerk[...]
    packed[0:3, :] = pos[...] + span * (vel[...] + span * (a / 2.0 + span * j / 6.0))
    packed[3:6, :] = vel[...] + span * (a + span * j / 2.0)
    packed[6:7, :] = span
    packed[7:8, :] = mass[...]
    packed[8:11, :] = a
    packed[11:14, :] = j
    packed[14:16, :] = jnp.zeros((2, star_dev), F32)
    mine = packed.at[pl.ds(0, 8)]
    keep = pltpu.make_async_copy(mine, field.at[ia], load.at[7])
    keep.start()

    sister = (y * 2 + 1 - core, ja)
    field_copies = []
    for d in range(1, 4):
        peer = ((((y + d) % 4) * 2 + core), ja)
        c = push(mine, field.at[ia], field_send.at[d], field_recv.at[d], peer)
        c.start()
        field_copies.append(c)
    own_copy = push(mine, field.at[ia], field_send.at[0], field_recv.at[0], sister)
    own_copy.start()

    first = (ia * lax.axis_size("ja") + ja) * star_dev

    def send_part(d, e):
        dest, dest_x = (ia + d) % N_IA, (x + e) % N_X
        return push(
            outgoing.at[dest, dest_x], incoming.at[ia * N_X + x], part_send, part_recv,
            (dest, dest_x * N_Z + z),
        )

    def pick(d, carry):
        dest = (ia + d) % N_IA

        @pl.when(d > 0)
        def _():
            send_ids(N_IA - d).wait_recv()

        for b in range(N_X):
            spot = jnp.broadcast_to(ids[dest, :, 128 * b:128 * b + 128] - first, (8, 128))
            tile, lane = spot >> 7, spot & 127
            found = [jnp.zeros((8, 128), F32)] * 2
            for q in range(star_dev // 128):
                for h in range(2):
                    part = packed[8 * h:8 * h + 8, q * 128:q * 128 + 128]
                    got = jnp.take_along_axis(part, lane, axis=1, mode="promise_in_bounds")
                    found[h] = jnp.where(tile == q, got, found[h])
            for h in range(2):
                outgoing[dest, b, h] = found[h]
        for e in range(1, N_X):
            send_part(d, e).start()

        @pl.when(d > 0)
        def _():
            send_part(d, 0).start()

        return carry

    lax.fori_loop(0, N_IA, pick, 0)
    for d in range(1, N_IA):
        send_ids(d).wait_send()
    incoming[ia * N_X + x] = outgoing[ia, x]

    wait_all(incoming, N_IA * N_X - 1, part_send, part_recv, plane[0])
    total = incoming[0]
    for i in range(1, N_IA * N_X):
        total = total + incoming[i]
    forwards = []

    def hand_on():
        for c in field_copies:
            c.wait()
        for d in range(1, 4):
            origin = ((y + d) % 4) * 2 + core
            c = push(
                field.at[origin], field.at[origin], field_send.at[3 + d], field_recv.at[3 + d], sister
            )
            c.start()
            forwards.append(c)

    share_over_ja(x, z, total, along_x, along_z, from_z, state, ja_sems, hand_on)
    keep.wait()
    own_copy.wait()
    for c in forwards:
        c.wait()


def pair_kernel(state, field_in, sums, field, targets, stars, totals, load):
    blocks, _, width = field.shape
    chunks = stars.shape[0]
    per_chunk = CHUNK // width
    for i in range(blocks):
        pltpu.make_async_copy(field_in.at[i], field.at[i], load.at[i]).start()
    row_blocks = state.shape[0]

    for b in range(row_blocks):
        for j in range(6):
            row = state[b, 0, j:j + 1, :]
            turned = jnp.broadcast_to(row, (128, 128)).T
            for g in range(16):
                targets[b * 16 + g, j] = turned[8 * g:8 * g + 8]

    def prepare(chunk, carry):
        for part in range(per_chunk):
            index = chunk * per_chunk + part
            pltpu.make_async_copy(field_in.at[index], field.at[index], load.at[index]).wait()
            for j, source in enumerate((0, 1, 2, 3, 4, 5, 7)):
                row = field[index, source:source + 1, :]
                stars[chunk, j, :, part * width:(part + 1) * width] = jnp.broadcast_to(row, (8, width))
        return carry

    lax.fori_loop(0, chunks, prepare, 0)

    def group_sums(group, carry):
        here = [targets[group, j] for j in range(6)]

        def step(chunk, sofar):
            out = list(sofar)
            for t in range(CHUNK // 128):
                star = [stars[chunk, j, :, t * 128:t * 128 + 128] for j in range(7)]
                dx = [star[j] - here[j] for j in range(3)]
                du = [star[3 + j] - here[3 + j] for j in range(3)]
                dist = (dx[0] * dx[0] + dx[1] * dx[1]) + (dx[2] * dx[2] + soft_square)
                dot = dx[0] * du[0] + dx[1] * du[1] + dx[2] * du[2]
                root = lax.rsqrt(dist)
                square = pl.reciprocal(dist, approx=True)
                weight = star[6] * root
                cube = weight * square
                along = dot * square
                for j in range(3):
                    pull = cube * dx[j]
                    out[j] = out[j] + pull
                    out[3 + j] = out[3 + j] + cube * du[j]
                    out[6 + j] = out[6 + j] + along * pull
                out[9] = out[9] + weight
            return tuple(out)

        out = lax.fori_loop(0, chunks, step, (jnp.zeros((8, 128), F32),) * 10)
        b, row = group // 16, group % 16
        whole = list(out[0:3]) + [out[3 + j] - 3.0 * out[6 + j] for j in range(3)] + [out[9]]
        for j in range(7):
            totals[b, j, pl.ds(row * 8, 8), :] = whole[j]
        return carry

    lax.fori_loop(0, row_blocks * 16, group_sums, 0)

    for b in range(row_blocks):
        for j in range(7):
            sums[b, j:j + 1, :] = jnp.sum(totals[b, j].T, 0, keepdims=True)
        sums[b, 7:8, :] = jnp.zeros((1, 128), F32)


def finish_kernel(state, sums, corrected, potential, from_x, from_z, sems):
    ia, ja, x, z = place()
    along_x, along_z = ja_peers(ia, x, z)
    enter(along_x + along_z)
    from_z[z] = sums[...]
    for d in range(1, N_Z):
        push(from_z.at[z], from_z.at[z], sems.at[0], sems.at[1], along_z[d - 1]).start()
    wait_all(from_z, N_Z - 1, sems.at[0], sems.at[1], along_z[0])
    total = from_z[0]
    for i in range(1, N_Z):
        total = total + from_z[i]
    from_x[x] = total
    for d in range(1, N_X):
        push(from_x.at[x], from_x.at[x], sems.at[2], sems.at[3], along_x[d - 1]).start()
    wait_all(from_x, N_X - 1, sems.at[2], sems.at[3], along_x[0])
    full = from_x[0]
    for i in range(1, N_X):
        full = full + from_x[i]
    for b in range(N_X):
        lanes = slice(b * 128, b * 128 + 128)
        times = state[b, 0, 6:7, :]
        for j in range(3):
            accel_new = full[b, j:j + 1, :]
            jerk_new = full[b, 3 + j:4 + j, :]
            accel_gap = state[b, 1, j:j + 1, :] - accel_new
            jerk_prev = state[b, 1, 3 + j:4 + j, :]
            second = -6.0 * accel_gap - times * (4.0 * jerk_prev + 2.0 * jerk_new)
            third = 12.0 * accel_gap + 6.0 * times * (jerk_prev + jerk_new)
            corrected[j:j + 1, lanes] = state[b, 0, j:j + 1, :] + times * times * (second / 24.0 + third / 120.0)
            corrected[3 + j:4 + j, lanes] = state[b, 0, 3 + j:4 + j, :] + times * (second / 6.0 + third / 24.0)
            corrected[6 + j:7 + j, lanes] = accel_new
            corrected[9 + j:10 + j, lanes] = jerk_new
        potential[:, lanes] = state[b, 0, 7:8, :] * self_root - full[b, 6:7, :]


def local(position, velocity, acceleration, old_jerk, star_mass, elapsed, active):
    star_dev = position.shape[1]
    vmem = pl.BlockSpec(memory_space=pltpu.VMEM)
    hbm = pl.BlockSpec(memory_space=pltpu.HBM)
    dma = pltpu.SemaphoreType.DMA
    state, field = pl.pallas_call(
        gather_kernel,
        out_shape=(
            jax.ShapeDtypeStruct((N_X, 2, 8, 128), F32),
            jax.ShapeDtypeStruct((N_IA, 8, star_dev), F32),
        ),
        in_specs=[hbm] * 7,
        out_specs=(vmem, hbm),
        scratch_shapes=[
            pltpu.VMEM((3, star_dev), F32),
            pltpu.VMEM((3, star_dev), F32),
            pltpu.VMEM((3, star_dev), F32),
            pltpu.VMEM((3, star_dev), F32),
            pltpu.VMEM((1, star_dev), F32),
            pltpu.VMEM((1, star_dev), F32),
            pltpu.VMEM((1, 512), jnp.int32),
            pltpu.VMEM((N_IA, 1, 512), jnp.int32),
            pltpu.VMEM((16, star_dev), F32),
            pltpu.VMEM((N_IA, N_X, 2, 8, 128), F32),
            pltpu.VMEM((N_IA * N_X, 2, 8, 128), F32),
            pltpu.VMEM((N_Z, 2, 8, 128), F32),
            dma((8,)), dma((8,)), dma((8,)), dma, dma, dma((8,)), dma((8,)), dma((4,)),
        ],
        compiler_params=pltpu.CompilerParams(
            collective_id=0, has_side_effects=True, vmem_limit_bytes=56 << 20
        ),
        name="gather_targets",
    )(
        position, velocity, acceleration, old_jerk, star_mass.reshape(1, -1),
        elapsed.reshape(1, -1), active.reshape(1, -1),
    )
    chunks = N_IA * star_dev // CHUNK
    sums = pl.pallas_call(
        pair_kernel,
        out_shape=jax.ShapeDtypeStruct((N_X, 8, 128), F32),
        in_specs=[vmem, hbm],
        out_specs=vmem,
        scratch_shapes=[
            pltpu.VMEM((N_IA, 8, star_dev), F32),
            pltpu.VMEM((N_X * 16, 6, 8, 128), F32),
            pltpu.VMEM((chunks, 7, 8, CHUNK), F32),
            pltpu.VMEM((N_X, 7, 128, 128), F32),
            dma((N_IA,)),
        ],
        compiler_params=pltpu.CompilerParams(vmem_limit_bytes=60 << 20),
        name="pair_sums",
    )(state, field)
    corrected, potential = pl.pallas_call(
        finish_kernel,
        out_shape=(
            jax.ShapeDtypeStruct((12, 512), F32),
            jax.ShapeDtypeStruct((1, 512), F32),
        ),
        in_specs=[vmem] * 2,
        out_specs=(vmem, vmem),
        scratch_shapes=[
            pltpu.VMEM((N_X, N_X, 8, 128), F32),
            pltpu.VMEM((N_Z, N_X, 8, 128), F32),
            dma((4,)),
        ],
        compiler_params=pltpu.CompilerParams(
            collective_id=1, has_side_effects=True, vmem_limit_bytes=4 << 20
        ),
        name="reduce_and_correct",
    )(state, sums)
    return corrected, potential.reshape(-1)


def solution(mesh):
    placed = (
        P(None, ("ia", "ja")),
        P(None, ("ia", "ja")),
        P(None, ("ia", "ja")),
        P(None, ("ia", "ja")),
        P(("ia", "ja")),
        P(("ia", "ja")),
        P("ia"),
    )
    return jax.shard_map(
        local, mesh=mesh, in_specs=placed, out_specs=(P(None, "ia"), P("ia")), check_vma=False
    )
```

time: 672 us -> 141 us (0.21)
  blocking collectives: 245 us -> 0 us
  other arithmetic: 195 us -> 0 us
  waiting for transfers between devices: 159 us -> 0 us
  Pallas kernels: 0 us -> 136 us
  local copies, waits for them, and re-layouts: 55.7 us -> 1.91 us
  between operations: 14.2 us -> 0.68 us
    psum x2 -> x0, blocking collectives: 219 us -> none  [the longest x1 140 us: local(): lax.psum((accel_sum, jerk_sum, pot_sum), 'ja')]
    reduce_sum x192 -> x0, other arithmetic: 191 us -> none  [the longest x64 99.6 us: step_block(): jerk_sum = jnp.sum(cube[None] * (relvel - along[None] * offset), 2)]
    psum x1 -> x0, waiting for transfers between devices: 159 us -> none  [gather_all_state(): return lax.psum((picked, picked_span), ('ia', 'ja'))]
    pallas_call x0 -> x3, Pallas kernels: none -> 136 us  [the longest x1 94.5 us: local(): pl.pallas_call(pair_kernel, out_shape=jax.ShapeDtypeStruct((N_X, 8, 128),...]
    gather x3 -> x0, local copies, waits for them, and re-layouts: 39.4 us -> none  [the longest x1 23 us: local(): picked_span = jnp.where(owned_mask, jnp.take(elapsed, clipped), 0.0)]
    all_gather x2 -> x0, blocking collectives: 25.9 us -> none  [the longest x1 13.9 us: local(): piece = lax.all_gather(field, 'ia', axis=1, tiled=True)]
    slice x129 -> x0, local copies, waits for them, and re-layouts: 10.9 us -> none  [the longest x64 5.12 us: step_block(): weight = jnp.where(distinct, block[6][None, :] * inv_root, 0.0)]
  transfers between devices with their start and end apart: 1 -> 0, of which waited for: 1 -> 0; matrix products, arithmetic and copies ran while one was open for 0% -> 0% of each run, Pallas kernels for 0% -> 0%
where the time goes in v1:
time: 141 us; the launch traced here: 139 us
  Pallas kernels  136 us (96%)
  local copies, waits for them, and re-layouts  1.91 us (1%)
    pallas_call x1, Pallas kernels, local(): pl.pallas_call(pair_kernel, out_shape=jax.ShapeDtypeStruct((N_X, 8, 128),...  94.5 us
    pallas_call x1, Pallas kernels, local(): pl.pallas_call(gather_kernel, out_shape=(jax.ShapeDtypeStruct((N_X, 2, 8,...  29.6 us
    pallas_call x1, Pallas kernels, local(): pl.pallas_call(finish_kernel, out_shape=(jax.ShapeDtypeStruct((12, 512),...  12.4 us

profile of v1, /device:TPU:8, one launch (start us, length us, event | category | flops | bytes accessed | tf_op | source)
XLA Modules:
  0.0 139.1 jit_solution(6513843806037200772)
XLA Ops:
  0.6 29.6 %gather_targets.1 = (f32[4,2,8,128]{3,2,1,0:T(8,128)}, f32[8,8,4096]{2,1,0:T(8,128)}) custom-call(f32[3,4096]{1,0:T(4,128)} %pos_in.1, f32[3,4096]{1,0:T(4,128)} %vel_in.1, f32[3,4096]{1,0:T(4,128)} %acc_in.1, f32[3,4096]{1,0:T(4,128)} %jerk_in.1, f32[1,4096]{1,0:T(1,128)} %bitcast.5, f32[1,4096]{1,0:T(1,128)} %bitcast.6, s32[1,512]{1,0:T(1,128)} %bitcast.7), custom_call_target="tpu_custom_call" | custom-call | tf_op jit(solution)/shard_map/gather_targets/pallas_call | solution.py:308
  30.2 0.0 copy-start
  30.3 94.5 %pair_sums.1.sums = f32[4,8,128]{2,1,0:T(8,128)} custom-call(f32[4,2,8,128]{3,2,1,0:T(8,128)} %get-tuple-element.6.state, f32[8,8,4096]{2,1,0:T(8,128)} %get-tuple-element.7.field_in), custom_call_target="tpu_custom_call" | custom-call | tf_op jit(solution)/shard_map/pair_sums/pallas_call | solution.py:340
  124.8 0.0 copy-done
  124.8 0.0 copy-start.1
  124.8 0.7 copy-done.1
  125.5 12.4 %reduce_and_correct.1 = (f32[12,512]{1,0:T(8,128)S(1)}, f32[1,512]{1,0:T(1,128)S(1)}) custom-call(f32[4,2,8,128]{3,2,1,0:T(8,128)S(1)} %copy-done, f32[4,8,128]{2,1,0:T(8,128)S(1)} %copy-done.1), custom_call_target="tpu_custom_call" | custom-call | tf_op jit(solution)/shard_map/reduce_and_correct/pallas_call | solution.py:355
  137.9 0.6 copy.11
  138.5 0.6 copy.12
Async XLA Ops:
  30.2 94.5 %copy-start = (f32[4,2,8,128]{3,2,1,0:T(8,128)S(1)}, f32[4,2,8,128]{3,2,1,0:T(8,128)}, u32[]{:S(2)}) copy-start(f32[4,2,8,128]{3,2,1,0:T(8,128)} %get-tuple-element.6.state) | copy-start | bytes 98308
  124.8 0.7 copy-start.1
